TPU v7x, 32 devices: a whole 2x2x4 slice. The times are simulated.
32 devices in a mesh: dp: 8 (over y, x, core), blk: 4 (over z).
Axes of the slice: x: 2, y: 2, z: 4, core: 2. Of those that a mesh axis runs over, the one named last changes fastest.
Arguments:
- tokens: bfloat16 [24, 1024, 768], P('dp', 'blk'), may hold values from -6 to 6
- live_count: int32 [8], P('dp'), may hold values from 1 to 3, as said below
- first_gain: float32 [768], replicated, may hold values from 0.1 to 1.9
- first_shift: float32 [768], replicated, may hold values from -1.75 to 1.75
- joint_weight: bfloat16 [768, 2304], replicated, may hold values from -0.21875 to 0.21875
- query_bias: float32 [768], replicated, may hold values from -3 to 3
- value_bias: float32 [768], replicated, may hold values from -0.3125 to 0.3125
- out_weight: bfloat16 [768, 768], replicated, may hold values from -2.5 to 2.5
- out_bias: float32 [768], replicated, may hold values from -1.75 to 1.75
- second_gain: float32 [768], replicated, may hold values from 0.1 to 1.9
- second_shift: float32 [768], replicated, may hold values from -1.75 to 1.75
- up_weight: bfloat16 [768, 3072], replicated, may hold values from -0.21875 to 0.21875
- up_bias: float32 [3072], replicated, may hold values from -1.75 to 1.75
- down_weight: bfloat16 [3072, 768], replicated, may hold values from -0.109375 to 0.109375
- down_bias: float32 [768], replicated, may hold values from -1.75 to 1.75
- cotangent: bfloat16 [24, 1024, 768], P('dp', 'blk'), may hold values from -6 to 6
Outputs:
- output: bfloat16 [24, 1024, 768], P('dp', 'blk')
- grad_tokens: bfloat16 [24, 1024, 768], P('dp', 'blk')
- grad_first_gain: float32 [768], replicated
- grad_first_shift: float32 [768], replicated
- grad_joint_weight: float32 [768, 2304], replicated
- grad_query_bias: float32 [768], replicated
- grad_value_bias: float32 [768], replicated
- grad_out_weight: float32 [768, 768], replicated
- grad_out_bias: float32 [768], replicated
- grad_second_gain: float32 [768], replicated
- grad_second_shift: float32 [768], replicated
- grad_up_weight: float32 [768, 3072], replicated
- grad_up_bias: float32 [3072], replicated
- grad_down_weight: float32 [3072, 768], replicated
- grad_down_bias: float32 [768], replicated
Inputs may be any that keep to these rules, and one draw needn't show every extreme that they name: `live_count`: some index of dp has 3 live sequences and some other index has 1.
All inputs are finite; a program needn't handle non-finite values.
Results may differ from a plain program's by a relative error of at most 0.017.
Values may be sent and summed in bfloat16 or wider, within the bound.
No kernel may reach another device: no remote copies, remote signals or barrier semaphores. Data moves between devices by JAX's collectives and lax.ppermute only.
A program may use at most 256 MiB of HBM per device.

v0:
```python
from functools import partial
import math

import jax
import jax.numpy as jnp
from jax import lax
from jax.sharding import PartitionSpec as P

D = 768
HEADS = 12
HEAD_DIM = 64


NEG_FILL = -1e30
NORM_EPS = 1e-05


def layer_norm(values, norm_gain, norm_shift):
    center = values - jnp.mean(values, axis=-1, keepdims=True)
    spread = jnp.mean(center * center, axis=-1, keepdims=True)
    return center * lax.rsqrt(spread + NORM_EPS) * norm_gain + norm_shift


def rows_inner(first_op, second_op):
    return lax.dot_general(
        first_op, second_op, (((0,), (0,)), ((), ())), preferred_element_type=jnp.float32
    )


def times_transposed(first_op, second_op):
    return lax.dot_general(
        first_op, second_op, (((1,), (1,)), ((), ())), preferred_element_type=jnp.float32
    )


def as_heads(matrix, slot_count, block_rows):
    return matrix.reshape(slot_count, block_rows, HEADS, HEAD_DIM)


def fold_block(state, keys_part, values_part, key_start, query_heads, query_place, score_scale):
    slot_count, block_rows = (query_heads.shape[0], query_heads.shape[1])
    run_max, run_sum, run_acc = state
    key_heads = as_heads(keys_part, slot_count, block_rows)
    value_heads = as_heads(values_part, slot_count, block_rows)
    key_place = key_start + jnp.arange(block_rows, dtype=jnp.int32)
    causal = key_place[None, :] <= query_place[:, None]
    scores = (
        jnp.einsum("sqhd,skhd->shqk", query_heads, key_heads, preferred_element_type=jnp.float32)
        * score_scale
    )
    scores = jnp.where(causal, scores, NEG_FILL)
    new_max = jnp.maximum(run_max, jnp.max(scores, axis=-1))
    unnormed = jnp.where(causal, jnp.exp(scores - new_max[..., None]), 0.0)
    factor = jnp.exp(run_max - new_max)
    run_sum = run_sum * factor + jnp.sum(unnormed, axis=-1)
    run_acc = run_acc * factor[..., None] + jnp.einsum(
        "shqk,skhd->shqd",
        unnormed.astype(jnp.bfloat16),
        value_heads,
        preferred_element_type=jnp.float32,
    )
    return (new_max, run_sum, run_acc)


def fold_keys(state, pieces, first_row, query_heads, query_place, score_scale):
    keys_all, values_all = pieces
    block_rows = query_heads.shape[1]

    def key_step(block_index, carried):
        offset = block_index * block_rows
        keys_part = lax.dynamic_slice_in_dim(keys_all, offset, block_rows, 1)
        values_part = lax.dynamic_slice_in_dim(values_all, offset, block_rows, 1)
        return fold_block(
            carried, keys_part, values_part, offset, query_heads, query_place, score_scale
        )

    return lax.fori_loop(0, keys_all.shape[1] // block_rows, key_step, state)


def on_device(
    tokens,
    live_count,
    first_gain,
    first_shift,
    joint_weight,
    query_bias,
    value_bias,
    out_weight,
    out_bias,
    second_gain,
    second_shift,
    up_weight,
    up_bias,
    down_weight,
    down_bias,
    cotangent,
):
    slot_count, block_rows = (tokens.shape[0], tokens.shape[1])
    row_total = slot_count * block_rows
    score_scale = 1.0 / math.sqrt(HEAD_DIM)
    flat_rows = tokens.astype(jnp.float32).reshape(row_total, D)
    live_slots = (jnp.arange(slot_count, dtype=jnp.int32) < live_count[0]).astype(jnp.float32)
    live_rows = jnp.repeat(live_slots, block_rows)[:, None]
    query_place = lax.axis_index("blk") * block_rows + jnp.arange(block_rows, dtype=jnp.int32)
    first_norm, first_pull = jax.vjp(layer_norm, flat_rows, first_gain, first_shift)
    attn_in = first_norm.astype(jnp.bfloat16)
    joined = jnp.dot(attn_in, joint_weight, preferred_element_type=jnp.float32)
    query_low = (joined[:, :D] + query_bias).astype(jnp.bfloat16)
    key_low = joined[:, D : 2 * D].astype(jnp.bfloat16)
    value_low = (joined[:, 2 * D :] + value_bias).astype(jnp.bfloat16)
    query_heads = as_heads(query_low, slot_count, block_rows)
    key_slab = key_low.reshape(slot_count, block_rows, D)
    value_slab = value_low.reshape(slot_count, block_rows, D)
    start_state = (
        jnp.full((slot_count, HEADS, block_rows), NEG_FILL, jnp.float32),
        jnp.zeros((slot_count, HEADS, block_rows), jnp.float32),
        jnp.zeros((slot_count, HEADS, block_rows, HEAD_DIM), jnp.float32),
    )
    folder = partial(
        fold_keys, query_heads=query_heads, query_place=query_place, score_scale=score_scale
    )
    run_max, run_sum, run_acc = folder(
        start_state,
        (
            lax.all_gather(key_slab, "blk", axis=1, tiled=True),
            lax.all_gather(value_slab, "blk", axis=1, tiled=True),
        ),
        jnp.int32(0),
    )
    mixed_full = run_acc / run_sum[..., None]
    log_total = run_max + jnp.log(run_sum)
    mixed_low = jnp.transpose(mixed_full, (0, 2, 1, 3)).reshape(row_total, D).astype(jnp.bfloat16)
    branch = jnp.dot(mixed_low, out_weight, preferred_element_type=jnp.float32) + out_bias
    hidden = flat_rows + branch
    second_norm, second_pull = jax.vjp(layer_norm, hidden, second_gain, second_shift)
    mlp_in = second_norm.astype(jnp.bfloat16)
    pre_act = jnp.dot(mlp_in, up_weight, preferred_element_type=jnp.float32) + up_bias
    gelu_out, gelu_pull = jax.vjp(partial(jax.nn.gelu, approximate=True), pre_act)
    active = gelu_out.astype(jnp.bfloat16)
    result = hidden + jnp.dot(active, down_weight, preferred_element_type=jnp.float32) + down_bias
    output = (result * live_rows).astype(jnp.bfloat16).reshape(tokens.shape)
    grad_result = cotangent.astype(jnp.float32).reshape(row_total, D) * live_rows
    grad_down_low = grad_result.astype(jnp.bfloat16)
    grad_down_bias = jnp.sum(grad_down_low.astype(jnp.float32), axis=0)
    grad_down_weight = rows_inner(active, grad_down_low)
    grad_active = times_transposed(grad_down_low, down_weight).astype(jnp.bfloat16)
    grad_pre = gelu_pull(grad_active.astype(jnp.float32))[0].astype(jnp.bfloat16)
    grad_up_bias = jnp.sum(grad_pre.astype(jnp.float32), axis=0)
    grad_up_weight = rows_inner(mlp_in, grad_pre)
    grad_mlp_in = times_transposed(grad_pre, up_weight)
    grad_hidden_part, grad_second_gain, grad_second_shift = second_pull(grad_mlp_in)
    grad_hidden = grad_result + grad_hidden_part
    grad_branch = grad_hidden.astype(jnp.bfloat16)
    grad_out_bias = jnp.sum(grad_branch.astype(jnp.float32), axis=0)
    grad_out_weight = rows_inner(mixed_low, grad_branch)
    grad_mixed = times_transposed(grad_branch, out_weight).astype(jnp.bfloat16)
    grad_mixed_heads = as_heads(grad_mixed, slot_count, block_rows)
    row_delta = jnp.einsum("sqhd,shqd->shq", grad_mixed_heads.astype(jnp.float32), mixed_full)
    keys_back, values_back = (
        lax.all_gather(key_slab, "blk", axis=1, tiled=True),
        lax.all_gather(value_slab, "blk", axis=1, tiled=True),
    )

    def back_block(grad_query_acc, block_index):
        offset = block_index * block_rows
        key_heads = as_heads(
            lax.dynamic_slice_in_dim(keys_back, offset, block_rows, 1), slot_count, block_rows
        )
        value_heads = as_heads(
            lax.dynamic_slice_in_dim(values_back, offset, block_rows, 1), slot_count, block_rows
        )
        key_place = offset + jnp.arange(block_rows, dtype=jnp.int32)
        causal = key_place[None, :] <= query_place[:, None]
        scores = (
            jnp.einsum(
                "sqhd,skhd->shqk", query_heads, key_heads, preferred_element_type=jnp.float32
            )
            * score_scale
        )
        probs_full = jnp.where(causal, jnp.exp(scores - log_total[..., None]), 0.0)
        grad_probs = jnp.einsum(
            "sqhd,skhd->shqk", grad_mixed_heads, value_heads, preferred_element_type=jnp.float32
        )
        grad_scores = (probs_full * (grad_probs - row_delta[..., None])).astype(jnp.bfloat16)
        grad_query_acc = grad_query_acc + jnp.einsum(
            "shqk,skhd->sqhd", grad_scores, key_heads, preferred_element_type=jnp.float32
        )
        grad_value = jnp.einsum(
            "shqk,sqhd->skhd",
            probs_full.astype(jnp.bfloat16),
            grad_mixed_heads,
            preferred_element_type=jnp.float32,
        )
        grad_key = (
            jnp.einsum(
                "shqk,sqhd->skhd", grad_scores, query_heads, preferred_element_type=jnp.float32
            )
            * score_scale
        )
        return (
            grad_query_acc,
            (
                grad_key.reshape(slot_count, block_rows, D),
                grad_value.reshape(slot_count, block_rows, D),
            ),
        )

    query_zero = jnp.zeros((slot_count, block_rows, HEADS, HEAD_DIM), jnp.float32)
    grad_query_sum, block_terms = lax.scan(
        back_block, query_zero, jnp.arange(lax.axis_size("blk"), dtype=jnp.int32)
    )
    key_summed, value_summed = (
        lax.psum_scatter(
            block_terms[0].astype(jnp.bfloat16), "blk", scatter_dimension=0, tiled=True
        ).astype(jnp.float32),
        lax.psum_scatter(
            block_terms[1].astype(jnp.bfloat16), "blk", scatter_dimension=0, tiled=True
        ).astype(jnp.float32),
    )
    grad_query_low = (grad_query_sum * score_scale).reshape(row_total, D).astype(jnp.bfloat16)
    grad_key_low = key_summed.reshape(row_total, D).astype(jnp.bfloat16)
    grad_value_low = value_summed.reshape(row_total, D).astype(jnp.bfloat16)
    grad_joined = jnp.concatenate([grad_query_low, grad_key_low, grad_value_low], axis=1)
    grad_query_bias = jnp.sum(grad_query_low.astype(jnp.float32), axis=0)
    grad_value_bias = jnp.sum(grad_value_low.astype(jnp.float32), axis=0)
    grad_joint_weight = rows_inner(attn_in, grad_joined)
    grad_attn_in = times_transposed(grad_joined, joint_weight)
    grad_flat_part, grad_first_gain, grad_first_shift = first_pull(grad_attn_in)
    grad_tokens = (grad_hidden + grad_flat_part).astype(jnp.bfloat16).reshape(tokens.shape)
    summed = tuple(
        lax.psum(
            (
                grad_first_gain,
                grad_first_shift,
                grad_joint_weight,
                grad_query_bias,
                grad_value_bias,
                grad_out_weight,
                grad_out_bias,
                grad_second_gain,
                grad_second_shift,
                grad_up_weight,
                grad_up_bias,
                grad_down_weight,
                grad_down_bias,
            ),
            ("dp", "blk"),
        )
    )
    return (output, grad_tokens) + summed


def solution(mesh):
    in_specs = (
        P("dp", "blk", None),
        P("dp"),
        P(),
        P(),
        P(),
        P(),
        P(),
        P(),
        P(),
        P(),
        P(),
        P(),
        P(),
        P(),
        P(),
        P("dp", "blk", None),
    )
    out_specs = (
        P("dp", "blk", None),
        P("dp", "blk", None),
        P(),
        P(),
        P(),
        P(),
        P(),
        P(),
        P(),
        P(),
        P(),
        P(),
        P(),
        P(),
        P(),
    )
    return jax.shard_map(
        on_device, mesh=mesh, in_specs=in_specs, out_specs=out_specs, check_vma=False
    )
```

profile of v0, /device:TPU:0, one launch (start us, length us, event | category | flops | bytes accessed | tf_op | source)
XLA Modules:
  0.0 1059.2 jit_solution(12353846891823542497)
XLA Ops:
  31.2 4.7 reshape.213
  43.0 71.5 %all-gather.3.cloned.1.call-done = bf16[3,1024,768]{1,2,0:T(8,128)(2,1)} async-done(((bf16[3,256,768]{1,2,0:T(8,128)(2,1)}), bf16[3,1024,768]{1,2,0:T(8,128)(2,1)}) %all-gather.3.cloned.1.call-update) | async-done | bytes 4718608 | tf_op jit(solution)/shard_map/all_gather | solution.py:125
  114.6 88.9 %all-gather.5.cloned.1.call-done = bf16[3,1024,768]{1,2,0:T(8,128)(2,1)} async-done(((bf16[3,256,768]{1,2,0:T(8,128)(2,1)}), bf16[3,1024,768]{1,2,0:T(8,128)(2,1)}) %all-gather.5.cloned.1.call-update) | async-done | bytes 4718608 | tf_op jit(solution)/shard_map/all_gather | solution.py:126
  203.5 41.4 %while.33 = (s32[]{:T(128)}, f32[3,12,256]{2,1,0:T(8,128)}, f32[3,12,256]{2,1,0:T(8,128)}, f32[3,12,256,64]{2,3,1,0:T(8,128)}, bf16[3,1024,768]{1,2,0:T(8,128)(2...) while((s32[]{:T(128)}, f32[3,12,256]{2,1,0:T(8,128)}, ...), condition=%wide.region_5.6_spmd.clone, body=%wide.region_2.5_spmd.clone.sunk | while | flops 636532224 | bytes 66179432 | solution.py:77
  252.2 6.6 fusion.59
  258.8 12.2 %convert_reduce_fusion = (f32[3072]{0:T(1024)}, bf16[768,3072]{1,0:T(8,128)(2,1)S(1)}) fusion(f32[768,3072]{1,0:T(8,128)} %fusion.59, f32[3072]{0:T(1024)S(1)} %copy-done.60, bf16[768,768]{1,0:T(8,128)(2,1)S(1)} %copy-done.27, bf16[3072,768]{1,0:T(8,128)(2,1)S(1)} %bitcast.206), kind=kOutput, calls=%fused_computation.57 | convolution fusion | flops 3682857984 | bytes 20078592 | tf_op jit(solution)/shard_map/dot_general | solution.py:31
  271.0 4.8 multiply_reduce_fusion.1
  293.4 121.8 %while.34 = (s32[]{:T(128)}, f32[3,256,12,64]{1,3,2,0:T(8,128)}, bf16[4,3,256,768]{3,2,1,0:T(8,128)(2,1)}, bf16[4,3,256,768]{3,2,1,0:T(8,128)(2,1)}, s32[4]{0:T(...) while((s32[]{:T(128)}, f32[3,256,12,64]{1,3,2,0:T(8,128)}, ...), condition=%wide.region_11.12_spmd.clone, body=%wide.region_10.11_spmd.clone.sunk | while | flops 1535967744 | bytes 110313912 | solution.py:209
  310.2 5.2 bitcast_add_fusion.3
  333.1 4.7 fusion.138
  340.1 5.9 bitcast_add_fusion.3
  370.7 5.9 bitcast_add_fusion.3
  401.3 5.9 bitcast_add_fusion.3
  423.6 7.5 fusion.58
  431.1 8.4 fusion.60
  439.5 59.4 %reduce-scatter.3.cloned.1.call-done = bf16[1,3,256,768]{3,2,1,0:T(8,128)(2,1)} async-done(((bf16[4,3,256,768]{3,2,1,0:T(8,128)(2,1)}), bf16[1,3,256,768]{3,2,1,0:T(8,128)(2,1)}) %reduce-scatter.3.cloned.1.call-update) | async-done | bytes 1179664 | tf_op jit(solution)/shard_map/reduce_scatter | solution.py:213
  501.3 85.6 %reduce-scatter.5.cloned.1.call-done = bf16[1,3,256,768]{3,2,1,0:T(8,128)(2,1)} async-done(((bf16[4,3,256,768]{3,2,1,0:T(8,128)(2,1)}), bf16[1,3,256,768]{3,2,1,0:T(8,128)(2,1)}) %reduce-scatter.5.cloned.1.call-update) | async-done | bytes 1179664 | tf_op jit(solution)/shard_map/reduce_scatter | solution.py:216
  589.3 8.3 fusion.51
  601.1 12.5 %multiply_convert_fusion.3 = bf16[768,768]{1,0:T(8,128)(2,1)} fusion(f32[768,768]{1,0:T(8,128)} %copy-done.8, bf16[3072,768]{1,0:T(8,128)(2,1)} %param.33, f32[768]{0:T(1024)S(1)} %copy-done.45, f32[768]{0:T(1024)} %param.34, f32[768,3072]{1,0:T(8,128)} %fusion.59, f32[3072]{0:T(1024)} %param.32), kind=kOutput, calls=%fused_computation.95 | convolution fusion | flops 3649830912 | bytes 17713152 | tf_op jit(solution)/shard_map/dot_general | solution.py:140
  620.3 44.2 %all-reduce = (f32[768]{0:T(1024)}, f32[768]{0:T(1024)}, f32[768]{0:T(1024)}, f32[768]{0:T(1024)}, f32[768]{0:T(1024)}, /*index=5*/f32[768]{0:T(1024)}, f32[768]{0:T(1024)}, f32[3072]{0:T(1024)}, f32[768]{0:T(1024)}) all-reduce(f32[768]{0:T(1024)} %get-tuple-element.340, ...), channel_id=1, replica_groups=mesh['dp'=8,'blk'=4] {'dp','blk'}, use_global_device_ids=true, to_apply=%region_17.18 | all-reduce | flops 9216 | bytes 73728 | tf_op jit(solution)/shard_map/psum | solution.py:231
  665.2 5.4 add_convert_fusion
  670.6 360.9 %all-reduce.4.cloned.1.call-done = (f32[768,2304]{1,0:T(8,128)}, f32[768,768]{1,0:T(8,128)}, f32[768,3072]{1,0:T(8,128)}, f32[3072,768]{1,0:T(8,128)}) async-done(((f32[768,2304]{1,0:T(8,128)}, f32[768,768]{1,0:T(8,128)}, f32[768,3072]{1,0:T(8,128)}, f32[3072,768]{1,0:T(8,128)}), (f32[768,2304]{1,0:T(8,128)}, f32[768,768]{1,0:T(8,128)}, f32[768,3072]{1,0:T(8,128)}, ...) | async-done | bytes 28311568 | tf_op jit(solution)/shard_map/psum | solution.py:231
  1031.4 6.6 copy.127
  1039.4 9.3 copy.129
  (388 shorter events, 216.2 us)
Async XLA Ops:
  7.2 107.4 %all-gather.3.cloned.1.call-start = ((), (), s32[]{:S(2)}) async-start(), calls=%async_computation.2 | async-start | bytes 5898240 | tf_op jit(solution)/shard_map/all_gather | solution.py:125
  22.6 180.9 %all-gather.5.cloned.1.call-start = ((), (), s32[]{:S(2)}) async-start(), calls=%async_computation.3 | async-start | bytes 5898240 | tf_op jit(solution)/shard_map/all_gather | solution.py:126
  29.2 469.7 %reduce-scatter.3.cloned.1.call-start = ((), (), s32[]{:S(2)}) async-start(), calls=%async_computation.4 | async-start | bytes 5898240 | tf_op jit(solution)/shard_map/reduce_scatter | solution.py:213
  31.2 245.6 %copy-start.44 = (f32[768]{0:T(1024)}, f32[768]{0:T(1024)S(1)}, u32[]{:S(2)}) copy-start(f32[768]{0:T(1024)S(1)} %mul.256) | copy-start | bytes 9220
  248.5 10.3 slice-start.7
  249.8 26.0 %copy-start.8 = (f32[768,768]{1,0:T(8,128)}, f32[768,768]{1,0:T(8,128)S(1)}, u32[]{:S(2)}) copy-start(f32[768,768]{1,0:T(8,128)S(1)} %get-tuple-element.417) | copy-start | bytes 7077892
  415.3 171.6 %reduce-scatter.5.cloned.1.call-start = ((), (), s32[]{:S(2)}) async-start(), calls=%async_computation.5 | async-start | bytes 5898240 | tf_op jit(solution)/shard_map/reduce_scatter | solution.py:216
  415.9 615.5 %all-reduce.4.cloned.1.call-start = ((), (), s32[]{:S(2)}) async-start(), calls=%async_computation.6 | async-start | bytes 56623104 | tf_op jit(solution)/shard_map/psum | solution.py:231
  415.9 7.6 slice-start.3
  421.0 10.1 slice-start.9
  423.6 7.5 copy-start.28
  423.6 7.5 copy-start.61
  423.6 7.5 slice-start.10
  423.6 7.5 slice-start.11
  601.0 12.6 %copy-start.20 = (bf16[1,3,256,768]{3,2,1,0:T(8,128)(2,1)S(1)}, bf16[1,3,256,768]{3,2,1,0:T(8,128)(2,1)}, u32[]{:S(2)}) copy-start(bf16[1,3,256,768]{3,2,1,0:T(8,128)(2,1)} %reduce-scatter.5.cloned.1.call-done) | copy-start | bytes 3538948
  601.0 13.4 %copy-start.7 = (bf16[3,256,768]{2,1,0:T(8,128)(2,1)S(1)}, bf16[3,256,768]{2,1,0:T(8,128)(2,1)}, u32[]{:S(2)}) copy-start(bf16[3,256,768]{2,1,0:T(8,128)(2,1)} %param.20) | copy-start | bytes 3538948
  601.0 13.4 %copy-start.29 = (bf16[768,768]{0,1:T(8,128)(2,1)S(1)}, bf16[768,768]{0,1:T(8,128)(2,1)}, u32[]{:S(2)}) copy-start(bf16[768,768]{0,1:T(8,128)(2,1)} %copy.55) | copy-start | bytes 3538948
  601.0 13.4 %copy-start.30 = (bf16[768,768]{0,1:T(8,128)(2,1)S(1)}, bf16[768,768]{0,1:T(8,128)(2,1)}, u32[]{:S(2)}) copy-start(bf16[768,768]{0,1:T(8,128)(2,1)} %copy.56) | copy-start | bytes 3538948
  601.1 13.4 %copy-start.36 = (bf16[96,8,3,256]{3,1,2,0:T(8,128)(2,1)S(1)}, bf16[96,8,3,256]{3,1,2,0:T(8,128)(2,1)}, u32[]{:S(2)}) copy-start(bf16[96,8,3,256]{3,1,2,0:T(8,128)(2,1)} %copy.90) | copy-start | bytes 3538948
  601.1 13.4 %copy-start.41 = (f32[768]{0:T(1024)S(1)}, f32[768]{0:T(1024)}, u32[]{:S(2)}) copy-start(f32[768]{0:T(1024)} %copy-done.40) | copy-start | bytes 9220
  601.1 13.4 %copy-start.49 = (f32[768]{0:T(1024)S(1)}, f32[768]{0:T(1024)}, u32[]{:S(2)}) copy-start(f32[768]{0:T(1024)} %param.22) | copy-start | bytes 9220
  1038.0 10.7 %slice-start = ((s8[9437184]{0:T(1024)(128)(4,1)}), s8[4194304]{0:T(1024)(128)(4,1)S(1)}, s32[]{:S(2)}) async-start(s8[9437184]{0:T(1024)(128)(4,1)} %bitcast.188), calls=%async_computation.7 | async-start | bytes 8388608
  1039.4 9.3 slice-start.1
  1039.4 9.3 slice-start.2
  (95 other events, 264.8 us)
Sparse Core Ops, SparseCore 0:
  22.7 91.8 all-gather.2
  116.1 87.3 all-gather.4
  415.4 83.4 reduce-scatter.2
  501.1 85.7 reduce-scatter.4
  597.7 433.7 all-reduce.3
where the time goes:
time: 1060 us
  waiting for transfers between devices  667 us (63%)
  matrix products  159 us (15%)
  local copies, waits for them, and re-layouts  127 us (12%)
  blocking collectives  44.2 us (4%)
  other arithmetic  43 us (4%)
  between operations  15.3 us (1%)
    psum x1, waiting for transfers between devices, on_device(): lax.psum((grad_first_gain, grad_first_shift, grad_joint_weight, grad_quer...  361 us
    all_gather x1, waiting for transfers between devices, on_device(): lax.all_gather(value_slab, 'blk', axis=1, tiled=True)  88.9 us
    reduce_scatter x1, waiting for transfers between devices, on_device(): lax.psum_scatter(block_terms[1].astype(jnp.bfloat16), 'blk', scatter_dime...  85.6 us
    all_gather x1, waiting for transfers between devices, on_device(): lax.all_gather(key_slab, 'blk', axis=1, tiled=True)  71.5 us
    reduce_scatter x1, waiting for transfers between devices, on_device(): lax.psum_scatter(block_terms[0].astype(jnp.bfloat16), 'blk', scatter_dime...  59.4 us
    psum x1, blocking collectives, on_device(): lax.psum((grad_first_gain, grad_first_shift, grad_joint_weight, grad_quer...  44.2 us
    unnamed x132, local copies, waits for them, and re-layouts  39.2 us
    dynamic_update_slice x12, local copies, waits for them, and re-layouts, on_device(): lax.scan(back_block, query_zero, jnp.arange(lax.axis_size('blk'), dtype=j...  31.9 us
  transfers between devices with their start and end apart: 5, of which 5 were waited for; matrix products, arithmetic and copies ran while one was open for 7% of the time, Pallas kernels for 0%

commit v1 on v0

v1 whole, which is shorter than its diff:
```python
import math
from functools import partial
import jax
import jax.numpy as jnp
from jax import lax
from jax.experimental import pallas as pl
from jax.experimental.pallas import tpu as pltpu
from jax.sharding import PartitionSpec as P

BF = jnp.bfloat16
F32 = jnp.float32
HEADS = 12
EPS = 1e-5
ROWS = 256
VMEM_LIMIT = 60 * 2**20


def params(**kw):
    return pltpu.CompilerParams(vmem_limit_bytes=VMEM_LIMIT, **kw)


def mm(a, b, ca, cb):
    return lax.dot_general(a, b, (((ca,), (cb,)), ((), ())), preferred_element_type=F32)


def shape(s, d):
    return jax.ShapeDtypeStruct(s, d)


def whole(s):
    n = len(s)
    return pl.BlockSpec(s, lambda *_: (0,) * n)


def norm_stats(t):
    c = t - jnp.mean(t, axis=-1, keepdims=True)
    r = lax.rsqrt(jnp.mean(c * c, axis=-1, keepdims=True) + EPS)
    return c * r, r


def joint_kernel(x_ref, g_ref, s_ref, w_ref, b_ref, a_ref, q_ref):
    j = pl.program_id(0)
    d = x_ref.shape[1]

    @pl.when(j == 0)
    def _():
        for i in range(x_ref.shape[0] // ROWS):
            rows = pl.ds(i * ROWS, ROWS)
            n, _ = norm_stats(x_ref[rows, :].astype(F32))
            a_ref[rows, :] = (n * g_ref[...] + s_ref[...]).astype(BF)

    scale = jnp.where(j == 0, 0.125, 1.0).astype(BF)
    for i in range(x_ref.shape[0] // ROWS):
        rows = pl.ds(i * ROWS, ROWS)
        q_ref[rows, :] = (mm(a_ref[rows, :], w_ref[...], 1, 0) + b_ref[...]).astype(BF) * scale


def joint_call(x, gain, shift, w, bias):
    L, d = x.shape
    return pl.pallas_call(
        joint_kernel,
        grid=(3,),
        in_specs=[whole((L, d)), whole((1, d)), whole((1, d)),
                  pl.BlockSpec((d, d), lambda j: (0, j)), pl.BlockSpec((1, d), lambda j: (0, j))],
        out_specs=[whole((L, d)), pl.BlockSpec((L, d), lambda j: (0, j))],
        out_shape=[shape((L, d), BF), shape((L, 3 * d), BF)],
        compiler_params=params(),
        name="joint",
    )(x, gain, shift, w, bias)


def attend_kernel(q_ref, k_ref, v_ref, o_ref, p_ref):
    L = q_ref.shape[0]
    lane = lax.broadcasted_iota(jnp.int32, (ROWS, 128), 1)
    row = lax.broadcasted_iota(jnp.int32, (ROWS, ROWS), 0)
    col = lax.broadcasted_iota(jnp.int32, (ROWS, ROWS), 1)
    tri = col <= row
    for i in range(L // ROWS):
        rows = pl.ds(i * ROWS, ROWS)
        q = q_ref[rows, :]
        outs = []
        for h in range(2):
            mine = (lane < 64) if h == 0 else (lane >= 64)
            qh = jnp.where(mine, q, jnp.zeros_like(q))
            s_diag = jnp.where(tri, mm(qh, k_ref[rows, :], 1, 1), -1e30)
            m = jnp.max(s_diag, axis=-1, keepdims=True)
            if i:
                prev = pl.ds(0, i * ROWS)
                s_prev = mm(qh, k_ref[prev, :], 1, 1)
                m = jnp.maximum(m, jnp.max(s_prev, axis=-1, keepdims=True))
                e_prev = jnp.exp(s_prev - m)
                total = jnp.sum(e_prev, axis=-1, keepdims=True)
            e_diag = jnp.exp(s_diag - m)
            t_diag = jnp.sum(e_diag, axis=-1, keepdims=True)
            total = total + t_diag if i else t_diag
            inv = 1.0 / total
            p_diag = (e_diag * inv).astype(BF)
            p_ref[h, rows, rows] = p_diag
            acc = mm(p_diag, v_ref[rows, :], 1, 0)
            if i:
                p_prev = (e_prev * inv).astype(BF)
                p_ref[h, rows, prev] = p_prev
                acc += mm(p_prev, v_ref[prev, :], 1, 0)
            outs.append(acc)
        o_ref[rows, :] = jnp.where(lane < 64, outs[0], outs[1]).astype(BF)


def attend_call(qkv):
    L, d3 = qkv.shape
    n = d3 // 3 // 128
    col = lambda k: pl.BlockSpec((L, 128), lambda j: (0, k * n + j))
    return pl.pallas_call(
        attend_kernel,
        grid=(n,),
        in_specs=[col(0), col(1), col(2)],
        out_specs=[col(0), pl.BlockSpec((2, L, L), lambda j: (j, 0, 0))],
        out_shape=[shape((L, d3 // 3), BF), shape((2 * n, L, L), BF)],
        compiler_params=params(),
        name="attend",
    )(qkv, qkv, qkv)


def out_kernel(m_ref, w_ref, b_ref, x_ref, g_ref, s_ref, h_ref, a_ref):
    h = x_ref[...].astype(F32) + mm(m_ref[...], w_ref[...], 1, 0) + b_ref[...]
    h_ref[...] = h
    n, _ = norm_stats(h)
    a_ref[...] = (n * g_ref[...] + s_ref[...]).astype(BF)


def out_call(mixed, w, b, x, gain, shift):
    L, d = x.shape
    blk = pl.BlockSpec((ROWS, d), lambda i: (i, 0))
    return pl.pallas_call(
        out_kernel,
        grid=(L // ROWS,),
        in_specs=[blk, whole((d, d)), whole((1, d)), blk, whole((1, d)), whole((1, d))],
        out_specs=[blk, blk],
        out_shape=[shape((L, d), F32), shape((L, d), BF)],
        compiler_params=params(),
        name="out_proj",
    )(mixed, w, b, x, gain, shift)


GC = math.sqrt(2.0 / math.pi)


def gelu_both(u):
    u2 = u * u
    t = jnp.tanh(u * (GC + GC * 0.044715 * u2))
    half = 0.5 + 0.5 * t
    return u * half, half + u * (0.5 - 0.5 * t * t) * (GC + 3 * GC * 0.044715 * u2)


def mlp_kernel(first, a_ref, c_ref, up_ref, ub_ref, dn_ref, *rest):
    if first:
        unit_ref, gb_ref, r_ref, e_ref, act, gpre = rest
    else:
        r0_ref, e0_ref, unit_ref, gb_ref, r_ref, e_ref, act, gpre = rest
    j = pl.program_id(0)
    L = a_ref.shape[0]
    gb = jnp.zeros(gb_ref.shape, F32)
    for i in range(L // ROWS):
        rows = pl.ds(i * ROWS, ROWS)
        u = mm(a_ref[rows, :], up_ref[...], 1, 0) + ub_ref[...]
        ga = mm(c_ref[rows, :], dn_ref[...], 1, 1).astype(BF)
        g, dg = gelu_both(u)
        act[rows, :] = g.astype(BF)
        gp = (ga.astype(F32) * dg).astype(BF)
        gpre[rows, :] = gp
        gb = gb + jnp.sum(gp.astype(F32), axis=0, keepdims=True)
    gb_ref[...] = gb
    unit_ref[0, 0] = mm(act[...], c_ref[...], 0, 0).astype(BF)
    unit_ref[0, 1] = mm(a_ref[...], gpre[...], 0, 0).astype(BF)

    @pl.when(j == 0)
    def _():
        for i in range(L // ROWS):
            rows = pl.ds(i * ROWS, ROWS)
            r = mm(act[rows, :], dn_ref[...], 1, 0)
            e = mm(gpre[rows, :], up_ref[...], 1, 1)
            if first:
                r_ref[rows, :] = r
                e_ref[rows, :] = e
            else:
                r_ref[rows, :] = r + r0_ref[rows, :]
                e_ref[rows, :] = e + e0_ref[rows, :]

    @pl.when(j > 0)
    def _():
        for i in range(L // ROWS):
            rows = pl.ds(i * ROWS, ROWS)
            r_ref[rows, :] += mm(act[rows, :], dn_ref[...], 1, 0)
            e_ref[rows, :] += mm(gpre[rows, :], up_ref[...], 1, 1)


def mlp_call(a, c, up, ub, dn, lo, tiles, tile, state=None):
    L, d = a.shape
    first = state is None
    at = lambda j: lo + j
    return pl.pallas_call(
        partial(mlp_kernel, first),
        grid=(tiles,),
        in_specs=[whole((L, d)), whole((L, d)),
                  pl.BlockSpec((d, tile), lambda j: (0, at(j))),
                  pl.BlockSpec((1, tile), lambda j: (0, at(j))),
                  pl.BlockSpec((tile, d), lambda j: (at(j), 0))]
        + ([] if first else [whole((L, d)), whole((L, d))]),
        out_specs=[pl.BlockSpec((1, 2, tile, d), lambda j: (j, 0, 0, 0)),
                   pl.BlockSpec((1, tile), lambda j: (0, j)),
                   whole((L, d)), whole((L, d))],
        out_shape=[shape((tiles, 2, tile, d), BF),
                   shape((1, tiles * tile), F32), shape((L, d), F32), shape((L, d), F32)],
        scratch_shapes=[pltpu.VMEM((L, tile), BF), pltpu.VMEM((L, tile), BF)],
        compiler_params=params(),
        name="mlp",
    )(a, c, up, ub, dn, *(() if first else state))


def norm_back(e, n, r):
    return r * (e - jnp.mean(e, axis=-1, keepdims=True) - n * jnp.mean(e * n, axis=-1, keepdims=True))


def middle_kernel(r_ref, e_ref, h_ref, c_ref, m_ref, w_ref, g_ref, db_ref, live_ref,
                  o_ref, gh_ref, gm_ref, dw_ref, sums_ref, acc):
    i = pl.program_id(0)

    @pl.when(i == 0)
    def _():
        acc[...] = jnp.zeros_like(acc)
        sums_ref[...] = jnp.zeros_like(sums_ref)

    h = h_ref[...]
    o_ref[...] = ((h + r_ref[...] + db_ref[...]) * live_ref[...]).astype(BF)
    n, r = norm_stats(h)
    e = e_ref[...]
    c = c_ref[...].astype(F32)
    gh = c + norm_back(e * g_ref[...], n, r)
    gh_ref[...] = gh
    gb = gh.astype(BF)
    gm_ref[...] = mm(gb, w_ref[...], 1, 1).astype(BF)
    acc[...] += mm(m_ref[...], gb, 0, 0)
    rows = lambda t: jnp.sum(t, axis=0, keepdims=True)
    sums_ref[0:1, :] += rows(e * n)
    sums_ref[1:2, :] += rows(e)
    sums_ref[2:3, :] += rows(gb.astype(F32))
    sums_ref[3:4, :] += rows(c)

    @pl.when(i == pl.num_programs(0) - 1)
    def _():
        dw_ref[...] = acc[...].astype(BF)


def middle_call(r, e, h, c, mixed, w, gain, down_bias, live):
    L, d = h.shape
    blk = pl.BlockSpec((ROWS, d), lambda i: (i, 0))
    return pl.pallas_call(
        middle_kernel,
        grid=(L // ROWS,),
        in_specs=[blk, blk, blk, blk, blk, whole((d, d)), whole((1, d)), whole((1, d)), whole((1, d))],
        out_specs=[blk, blk, blk, whole((d, d)), whole((8, d))],
        out_shape=[shape((L, d), BF), shape((L, d), F32), shape((L, d), BF), shape((d, d), BF), shape((8, d), F32)],
        scratch_shapes=[pltpu.VMEM((d, d), F32)],
        compiler_params=params(),
        name="middle",
    )(r, e, h, c, mixed, w, gain, down_bias, live)


def attend_back_kernel(q_ref, k_ref, v_ref, p_ref, g_ref, m_ref, dq_ref, dk_ref, dv_ref, dk_acc, dv_acc):
    L = q_ref.shape[0]
    lane = lax.broadcasted_iota(jnp.int32, (ROWS, 128), 1)
    low = lane < 64
    nb = L // ROWS
    for i in range(nb):
        rows = pl.ds(i * ROWS, ROWS)
        past = pl.ds(0, (i + 1) * ROWS)
        g = g_ref[rows, :]
        gm = g.astype(F32) * m_ref[rows, :].astype(F32)
        q = q_ref[rows, :]
        dqs, dks, dvs = [], [], []
        for h in range(2):
            mine = low if h == 0 else ~low
            gh = jnp.where(mine, g, jnp.zeros_like(g))
            delta = jnp.sum(jnp.where(mine, gm, 0.0), axis=-1, keepdims=True)
            p = p_ref[h, rows, past]
            dp = mm(gh, v_ref[past, :], 1, 1)
            ds = (p.astype(F32) * (dp - delta)).astype(BF)
            dqs.append(mm(ds, k_ref[past, :], 1, 0))
            dks.append(mm(ds, q, 0, 0))
            dvs.append(mm(p, g, 0, 0))
        dq_ref[rows, :] = (jnp.where(low, dqs[0], dqs[1]) * 0.125).astype(BF)
        lowp = lax.broadcasted_iota(jnp.int32, ((i + 1) * ROWS, 128), 1) < 64
        dk = jnp.where(lowp, dks[0], dks[1])
        dv = jnp.where(lowp, dvs[0], dvs[1])
        if i:
            prev = pl.ds(0, i * ROWS)
            dk_acc[prev, :] += dk[: i * ROWS]
            dv_acc[prev, :] += dv[: i * ROWS]
        dk_acc[rows, :] = dk[i * ROWS :]
        dv_acc[rows, :] = dv[i * ROWS :]
    dk_ref[...] = dk_acc[...].astype(BF)
    dv_ref[...] = dv_acc[...].astype(BF)


def attend_back_call(qkv, p, gm, mixed):
    L, d3 = qkv.shape
    n = d3 // 3 // 128
    col = lambda k: pl.BlockSpec((L, 128), lambda j: (0, k * n + j))
    s = shape((L, d3 // 3), BF)
    return pl.pallas_call(
        attend_back_kernel,
        grid=(n,),
        in_specs=[col(0), col(1), col(2), pl.BlockSpec((2, L, L), lambda j: (j, 0, 0)), col(0), col(0)],
        out_specs=[col(0)] * 3,
        out_shape=[s] * 3,
        scratch_shapes=[pltpu.VMEM((L, 128), F32), pltpu.VMEM((L, 128), F32)],
        compiler_params=params(),
        name="attend_back",
    )(qkv, qkv, qkv, p, gm, mixed)


def joint_weight_kernel(a_ref, q_ref, k_ref, v_ref, w_ref, sums_ref):
    d = a_ref.shape[1]
    sums_ref[...] = jnp.zeros_like(sums_ref)
    for n, ref in enumerate((q_ref, k_ref, v_ref)):
        w_ref[n] = mm(a_ref[...], ref[...], 0, 0).astype(BF)
    sums_ref[0:1, :] = jnp.sum(q_ref[...].astype(F32), axis=0, keepdims=True)
    sums_ref[1:2, :] = jnp.sum(v_ref[...].astype(F32), axis=0, keepdims=True)


def joint_weight_call(a, dq, dk, dv):
    L, d = a.shape
    return pl.pallas_call(
        joint_weight_kernel,
        out_shape=[shape((3, d, d), BF), shape((8, d), F32)],
        compiler_params=params(),
        name="joint_weight",
    )(a, dq, dk, dv)


def tokens_kernel(q_ref, k_ref, v_ref, w_ref, x_ref, gh_ref, g_ref, o_ref, sums_ref):
    i = pl.program_id(0)
    d = x_ref.shape[1]

    @pl.when(i == 0)
    def _():
        sums_ref[...] = jnp.zeros_like(sums_ref)

    e = mm(q_ref[...], w_ref[:, 0:d], 1, 1) + mm(k_ref[...], w_ref[:, d:2 * d], 1, 1) + mm(v_ref[...], w_ref[:, 2 * d:], 1, 1)
    n, r = norm_stats(x_ref[...].astype(F32))
    o_ref[...] = (gh_ref[...] + norm_back(e * g_ref[...], n, r)).astype(BF)
    sums_ref[0:1, :] += jnp.sum(e * n, axis=0, keepdims=True)
    sums_ref[1:2, :] += jnp.sum(e, axis=0, keepdims=True)


def tokens_call(dq, dk, dv, w, x, gh, gain):
    L, d = x.shape
    blk = pl.BlockSpec((ROWS, d), lambda i: (i, 0))
    return pl.pallas_call(
        tokens_kernel,
        grid=(L // ROWS,),
        in_specs=[blk, blk, blk, whole((d, 3 * d)), blk, blk, whole((1, d))],
        out_specs=[blk, whole((8, d))],
        out_shape=[shape((L, d), BF), shape((8, d), F32)],
        compiler_params=params(),
        name="tokens_back",
    )(dq, dk, dv, w, x, gh, gain)


def bits_of(count):
    assert count & (count - 1) == 0
    return count.bit_length() - 1


class Moves:
    def __init__(self, n_dp, n_blk, slots):
        assert slots <= n_blk
        self.n_dp, self.n_blk, self.slots = n_dp, n_blk, slots
        self.dp, self.blk = lax.axis_index("dp"), lax.axis_index("blk")
        self.odd = self.dp % 2

    def slot(self, blk):
        return jnp.where(self.odd == 1, self.n_blk - 1 - blk, blk)

    def perm(self, step, back):
        pairs = []
        for g in range(self.n_dp):
            for b in range(self.n_blk):
                d = (b + step) % self.n_blk
                s = self.n_blk - 1 - d if g % 2 else d
                if s < self.slots:
                    pair = (g * self.n_blk + b, g * self.n_blk + d)
                    pairs.append(pair[::-1] if back else pair)
        return pairs

    def gather(self, x):
        parts = []
        for step in range(self.n_blk):
            s = jnp.minimum(self.slot((self.blk + step) % self.n_blk), self.slots - 1)
            part = lax.dynamic_index_in_dim(x, s, 0, keepdims=False)
            if step:
                part = lax.ppermute(part, ("dp", "blk"), self.perm(step, False))
            parts.append(part)
        return parts

    def join(self, parts, scale=None):
        block, d = parts[0].shape
        out = jnp.zeros((self.n_blk, block, d), parts[0].dtype)
        for step, part in enumerate(parts):
            if scale is not None:
                part = part * scale
            out = lax.dynamic_update_index_in_dim(out, part, (self.blk - step) % self.n_blk, 0)
        return out.reshape(self.n_blk * block, d)

    def scatter(self, y):
        y = y.reshape(self.n_blk, -1, y.shape[-1])
        parts = []
        for step in range(self.n_blk):
            part = lax.dynamic_index_in_dim(y, (self.blk - step) % self.n_blk, 0, keepdims=False)
            if step:
                part = lax.ppermute(part, ("dp", "blk"), self.perm(step, True))
            parts.append(part)
        held = jnp.stack(parts)
        slots = []
        for s in range(self.slots):
            home = jnp.where(self.odd == 1, self.n_blk - 1 - s, s)
            slots.append(lax.dynamic_index_in_dim(held, (home - self.blk) % self.n_blk, 0, keepdims=False))
        return jnp.stack(slots)


def swap(x, n, bit):
    return lax.ppermute(x, ("dp", "blk"), [(i, i ^ (1 << bit)) for i in range(n)])


def sum_scatter(x, n, me, order):
    for bit in order:
        half = x.shape[0] // 2
        up = (me >> bit) & 1
        sent = lax.dynamic_slice_in_dim(x, (1 - up) * half, half, 0)
        kept = lax.dynamic_slice_in_dim(x, up * half, half, 0)
        x = kept + swap(sent, n, bit)
    return x


def spread(x, n, me, order):
    for bit in reversed(order):
        up = (me >> bit) & 1
        other = swap(x, n, bit)
        x = jnp.where(up == 0, jnp.stack([x, other]), jnp.stack([other, x])).reshape(2 * x.shape[0], x.shape[1])
    return x


def sum_small(x, n, order):
    for bit in order:
        x = x + swap(x, n, bit)
    return x


def on_device(n_dp, n_blk, tokens, live_count, first_gain, first_shift, joint_weight, query_bias, value_bias,
              out_weight, out_bias, second_gain, second_shift, up_weight, up_bias, down_weight, down_bias, cotangent):
    slots, block, d = tokens.shape
    n = n_dp * n_blk
    ff = up_weight.shape[1]
    tiles = ff // d
    moves = Moves(n_dp, n_blk, slots)
    me = moves.dp * n_blk + moves.blk
    row = lambda v: v.reshape(1, -1)
    mine = moves.slot(moves.blk)
    live = ((mine < slots) & (mine < live_count[0])).astype(F32)

    x = moves.join(moves.gather(tokens))
    c = moves.join(moves.gather(cotangent), live.astype(BF))

    bias = jnp.concatenate([query_bias, jnp.zeros((d,), F32), value_bias])
    attn_in, qkv = joint_call(x, row(first_gain), row(first_shift), joint_weight, row(bias))
    mixed, p = attend_call(qkv)
    hidden, mlp_in = out_call(mixed, out_weight, row(out_bias), x, row(second_gain), row(second_shift))

    low, dp_bits = bits_of(n_blk), bits_of(n_dp)
    core, plane = low, [low + 1 + i for i in range(dp_bits - 1)]
    orders = [[core] + plane + list(range(low)), [core] + plane[::-1] + list(range(low))]

    def all_sum(x):
        half = x.shape[0] // 2
        return [spread(sum_scatter(x[i * half : (i + 1) * half], n, me, o), n, me, o) for i, o in enumerate(orders)]

    state, downs, ups, up_biases = None, [], [], []
    per = tiles // 2
    for part in range(2):
        units, gb, r, e = mlp_call(mlp_in, c, up_weight, row(up_bias), down_weight, part * per, per, d, state)
        state = (r, e)
        got = jnp.concatenate(all_sum(units.reshape(-1, d))).reshape(units.shape)
        downs += [got[i, 0] for i in range(per)]
        ups += [got[i, 1] for i in range(per)]
        up_biases.append(gb.reshape(-1, d))
    out, gh, gm, dwo, sums2 = middle_call(r, e, hidden, c, mixed, out_weight, row(second_gain), row(down_bias),
                                          jnp.full((1, d), 1.0, F32) * live)
    output = moves.scatter(out)
    dq, dk, dv = attend_back_call(qkv, p, gm, mixed)
    dj, sums1 = joint_weight_call(attn_in, dq, dk, dv)
    got = jnp.concatenate(all_sum(jnp.concatenate([dwo[None], dj]).reshape(-1, d))).reshape(4, d, d)
    gx, sums0 = tokens_call(dq, dk, dv, joint_weight, x, gh, row(first_gain))
    grad_tokens = moves.scatter(gx)
    small = jnp.concatenate([sums0[:2], sums1[:2], sums2[:4]] + up_biases)
    small = sum_small(small, n, orders[0])
    wide = lambda v: v.astype(F32)
    return (output, grad_tokens, small[0], small[1], wide(jnp.concatenate([got[1], got[2], got[3]], axis=1)),
            small[2], small[3], wide(got[0]), small[6], small[4], small[5], wide(jnp.concatenate(ups, axis=1)),
            small[8:].reshape(-1), wide(jnp.concatenate(downs, axis=0)), small[7])


def solution(mesh):
    seq = P("dp", "blk", None)
    n_dp, n_blk = mesh.shape["dp"], mesh.shape["blk"]
    return jax.shard_map(
        partial(on_device, n_dp, n_blk), mesh=mesh,
        in_specs=(seq, P("dp")) + (P(),) * 13 + (seq,),
        out_specs=(seq, seq) + (P(),) * 13,
        check_vma=False,
    )
```

time: 1060 us -> 490 us (0.46)
  waiting for transfers between devices: 667 us -> 159 us
  matrix products: 159 us -> 0 us
  Pallas kernels: 0 us -> 146 us
  starting transfers between devices: 0.73 us -> 106 us
  local copies, waits for them, and re-layouts: 127 us -> 31.6 us
  blocking collectives: 44.2 us -> 0 us
  between operations: 15.3 us -> 3.32 us
    psum x1 -> x0, waiting for transfers between devices: 361 us -> none  [on_device(): lax.psum((grad_first_gain, grad_first_shift, grad_joint_weight, grad_quer...]
    all_gather x2 -> x0, waiting for transfers between devices: 160 us -> none  [the longest x1 88.9 us: on_device(): lax.all_gather(value_slab, 'blk', axis=1, tiled=True)]
    ppermute x0 -> x77, waiting for transfers between devices: none -> 159 us  [the longest x65 118 us: swap(): return lax.ppermute(x, ('dp', 'blk'), [(i, i ^ 1 << bit) for i in range(n)])]
    dot_general x40 -> x0, matrix products: 159 us -> none  [the longest x4 26.6 us: rows_inner(): lax.dot_general(first_op, second_op, (((0,), (0,)), ((), ())), preferred_...]
    pallas_call x0 -> x9, Pallas kernels: none -> 146 us  [the longest x2 49.9 us: mlp_call(): pl.pallas_call(partial(mlp_kernel, first), grid=(tiles,), in_specs=[whole...]
    reduce_scatter x2 -> x0, waiting for transfers between devices: 145 us -> none  [the longest x1 85.6 us: on_device(): lax.psum_scatter(block_terms[1].astype(jnp.bfloat16), 'blk', scatter_dime...]
    ppermute x0 -> x77, starting transfers between devices: none -> 106 us  [the longest x65 69 us: swap(): return lax.ppermute(x, ('dp', 'blk'), [(i, i ^ 1 << bit) for i in range(n)])]
    psum x1 -> x0, blocking collectives: 44.2 us -> none  [on_device(): lax.psum((grad_first_gain, grad_first_shift, grad_joint_weight, grad_quer...]
  transfers between devices with their start and end apart: 5 -> 77, of which waited for: 5 -> 44; matrix products, arithmetic and copies ran while one was open for 7% -> 9% of each run, Pallas kernels for 0% -> 9%
where the time goes in v1:
time: 490 us; the launch traced here: 483 us
  waiting for transfers between devices  159 us (32%)
  Pallas kernels  146 us (30%)
  starting transfers between devices  106 us (22%)
  other arithmetic  37 us (8%)
  local copies, waits for them, and re-layouts  31.6 us (6%)
    ppermute x65, waiting for transfers between devices, swap(): return lax.ppermute(x, ('dp', 'blk'), [(i, i ^ 1 << bit) for i in range(n)])  118 us
    ppermute x65, starting transfers between devices, swap(): return lax.ppermute(x, ('dp', 'blk'), [(i, i ^ 1 << bit) for i in range(n)])  69 us
    pallas_call x2, Pallas kernels, mlp_call(): pl.pallas_call(partial(mlp_kernel, first), grid=(tiles,), in_specs=[whole...  49.9 us
    pallas_call x1, Pallas kernels, attend_call(): pl.pallas_call(attend_kernel, grid=(n,), in_specs=[col(0), col(1), col(2)...  26.9 us
    ppermute x6, waiting for transfers between devices, gather(): part = lax.ppermute(part, ('dp', 'blk'), self.perm(step, False))  26.7 us
    pallas_call x1, Pallas kernels, attend_back_call(): pl.pallas_call(attend_back_kernel, grid=(n,), in_specs=[col(0), col(1), c...  24.8 us
    ppermute x6, starting transfers between devices, gather(): part = lax.ppermute(part, ('dp', 'blk'), self.perm(step, False))  18.5 us
    ppermute x6, starting transfers between devices, scatter(): part = lax.ppermute(part, ('dp', 'blk'), self.perm(step, True))  18.5 us
  transfers between devices with their start and end apart: 77, of which 44 were waited for; matrix products, arithmetic and copies ran while one was open for 9% of the time, Pallas kernels for 9%

profile of v1, /device:TPU:0, one launch (start us, length us, event | category | flops | bytes accessed | tf_op | source)
XLA Modules:
  0.0 483.1 jit_solution(8701608504071550951)
XLA Ops:
  2.9 5.1 %collective-permute-start.3 = (bf16[256,768]{1,0:T(8,128)(2,1)}, bf16[256,768]{1,0:T(8,128)(2,1)}, u32[]{:S(2)}, u32[]{:S(2)}) collective-permute-start(bf16[256,768]{1,0:T(8,128)(2,1)} %get-tuple-element.108), channel_id=1, source_target_pairs={{0,1},{1,2},{3,0},{4,5},{5,6},{6,7},{8,9},{9,10},{11,8},{12,13},{1... | collective-permute-start | bytes 1179656 | tf_op jit(solution)/shard_map/ppermute | solution.py:401
  15.9 5.5 %collective-permute-start.1 = (bf16[256,768]{1,0:T(8,128)(2,1)}, bf16[256,768]{1,0:T(8,128)(2,1)}, u32[]{:S(2)}, u32[]{:S(2)}) collective-permute-start(bf16[256,768]{1,0:T(8,128)(2,1)} %get-tuple-element.114), channel_id=1, source_target_pairs={{0,2},{2,0},{3,1},{4,6},{5,7},{7,5},{8,10},{10,8},{11,9},{12,14},{... | collective-permute-start | bytes 1179656 | tf_op jit(solution)/shard_map/ppermute | solution.py:401
  31.2 8.9 %collective-permute-done.4 = bf16[256,768]{1,0:T(8,128)(2,1)} collective-permute-done((bf16[256,768]{1,0:T(8,128)(2,1)}, bf16[256,768]{1,0:T(8,128)(2,1)}, u32[]{:S(2)}, u32[]{:S(2)}) %collective-permute-start.4) | collective-permute-done | bytes 393248 | tf_op jit(solution)/shard_map/ppermute | solution.py:401
  41.1 17.8 %collective-permute-done.1 = bf16[256,768]{1,0:T(8,128)(2,1)} collective-permute-done((bf16[256,768]{1,0:T(8,128)(2,1)}, bf16[256,768]{1,0:T(8,128)(2,1)}, u32[]{:S(2)}, u32[]{:S(2)}) %collective-permute-start.1) | collective-permute-done | bytes 393248 | tf_op jit(solution)/shard_map/ppermute | solution.py:401
  62.2 8.7 %joint.1 = (bf16[1024,768]{1,0:T(8,128)(2,1)}, bf16[1024,2304]{1,0:T(8,128)(2,1)}) custom-call(bf16[1024,768]{1,0:T(8,128)(2,1)} %bitcast.176, f32[1,768]{1,0:T(1,128)} %reshape.715.g_ref, f32[1,768]{1,0:T(1,128)} %reshape.716.s_ref, bf16[768,2304]{1,0:T(8,128)(2,1)} %w_ref.7, f32[1,2304]{1,0:T(1,128)} %reshape.717.b_ref), custom_call_target="tpu_custom_call" | custom-call | tf_op jit(solution)/shard_map/joint/pallas_call | solution.py:60
  70.9 26.9 %attend.1 = (bf16[1024,768]{1,0:T(8,128)(2,1)}, bf16[12,1024,1024]{2,1,0:T(8,128)(2,1)}) custom-call(bf16[1024,2304]{1,0:T(8,128)(2,1)} %get-tuple-element.41.q_ref.k_ref.v_ref, bf16[1024,2304]{1,0:T(8,128)(2,1)} %get-tuple-element.41.q_ref.k_ref.v_ref, bf16[1024,2304]{1,0:T(8,128)(2,1)} %get-tuple-element.41.q_ref.k_ref.v_ref), custom_call_target="tpu_custom_call" | custom-call | tf_op jit(solution)/shard_map/attend/pallas_call | solution.py:112
  97.8 5.9 %out_proj.1 = (f32[1024,768]{1,0:T(8,128)}, bf16[1024,768]{1,0:T(8,128)(2,1)}) custom-call(bf16[1024,768]{1,0:T(8,128)(2,1)} %get-tuple-element.42.m_ref, bf16[768,768]{1,0:T(8,128)(2,1)} %w_ref.6, f32[1,768]{1,0:T(1,128)} %reshape.718.b_ref, bf16[1024,768]{1,0:T(8,128)(2,1)} %bitcast.177, f32[1,768]{1,0:T(1,128)} %reshape.719.g_ref, f32[1,768]{1,0:T(1,128)} %reshape.720.s_ref), custom_call_target="tpu_custom_call" | custom-call | tf_op jit(solution)/shard_map/out_proj/pallas_call | solution.py:133
  103.7 23.9 %mlp.2 = (bf16[2,2,768,768]{3,2,1,0:T(8,128)(2,1)}, f32[1,1536]{1,0:T(1,128)}, f32[1024,768]{1,0:T(8,128)}, f32[1024,768]{1,0:T(8,128)}) custom-call(bf16[1024,768]{1,0:T(8,128)(2,1)} %get-tuple-element.43.a_ref, bf16[1024,768]{1,0:T(8,128)(2,1)} %bitcast.173, bf16[768,3072]{1,0:T(8,128)(2,1)} %up_ref.3, f32[1,3072]{1,0:T(1,128)} %bitcast.291, ...), custom_call_target="tpu_custom_call" | custom-call | tf_op jit(solution)/shard_map/mlp/pallas_call | solution.py:200
  127.7 25.9 %mlp.3 = (bf16[2,2,768,768]{3,2,1,0:T(8,128)(2,1)}, f32[1,1536]{1,0:T(1,128)}, f32[1024,768]{1,0:T(8,128)}, f32[1024,768]{1,0:T(8,128)}) custom-call(bf16[1024,768]{1,0:T(8,128)(2,1)} %get-tuple-element.43.a_ref, bf16[1024,768]{1,0:T(8,128)(2,1)} %bitcast.174, bf16[768,3072]{1,0:T(8,128)(2,1)} %up_ref.3, f32[1,3072]{1,0:T(1,128)} %bitcast.292, ...), custom_call_target="tpu_custom_call" | custom-call | tf_op jit(solution)/shard_map/mlp/pallas_call | solution.py:200
  154.2 11.2 %middle.1 = (bf16[1024,768]{1,0:T(8,128)(2,1)}, f32[1024,768]{1,0:T(8,128)}, bf16[1024,768]{1,0:T(8,128)(2,1)}, bf16[768,768]{1,0:T(8,128)(2,1)}, f32[8,768]{1,0:T(8,128)}) custom-call(f32[1024,768]{1,0:T(8,128)} %get-tuple-element.46.r_ref, f32[1024,768]{1,0:T(8,128)} %get-tuple-element.47.e_ref, f32[1024,768]{1,0:T(8,128)} %get-tuple-element.48.h_ref, ...), custom_call_target="tpu_custom_call" | custom-call | tf_op jit(solution)/shard_map/middle/pallas_call | solution.py:256
  167.8 5.5 %collective-permute-start.8 = (bf16[256,768]{1,0:T(8,128)(2,1)}, bf16[256,768]{1,0:T(8,128)(2,1)S(1)}, u32[]{:S(2)}, u32[]{:S(2)}) collective-permute-start(bf16[256,768]{1,0:T(8,128)(2,1)} %get-tuple-element.104), channel_id=1, source_target_pairs={{0,1},{1,2},{2,3},{7,4},{5,6},{6,7},{8,9},{9,10},{10,11},{15,12},{... | collective-permute-start | bytes 1179656 | tf_op jit(solution)/shard_map/ppermute | solution.py:420
  177.2 24.8 %attend_back.1 = (bf16[1024,768]{1,0:T(8,128)(2,1)}, bf16[1024,768]{1,0:T(8,128)(2,1)}, bf16[1024,768]{1,0:T(8,128)(2,1)}) custom-call(bf16[1024,2304]{1,0:T(8,128)(2,1)} %get-tuple-element.41.q_ref.k_ref.v_ref, bf16[1024,2304]{1,0:T(8,128)(2,1)} %get-tuple-element.41.q_ref.k_ref.v_ref, bf16[1024,2304]{1,0:T(8,128)(2,1)} %get-tuple-element.41.q_ref.k_ref.v_ref, ...), custom_call_target="tpu_custom_call" | custom-call | tf_op jit(solution)/shard_map/attend_back/pallas_call | solution.py:309
  202.0 9.8 %tokens_back.1 = (bf16[1024,768]{1,0:T(8,128)(2,1)}, f32[8,768]{1,0:T(8,128)}) custom-call(bf16[1024,768]{1,0:T(8,128)(2,1)} %get-tuple-element.52.q_ref, bf16[1024,768]{1,0:T(8,128)(2,1)} %get-tuple-element.53.k_ref, bf16[1024,768]{1,0:T(8,128)(2,1)} %get-tuple-element.54.v_ref, bf16[768,2304]{1,0:T(8,128)(2,1)} %w_ref.7, bf16[1024,768]{1,0:T(8,128)(2,1)} %bitcast.178, ...), custom_call_target="tpu_custom_call" | custom-call | tf_op jit(solution)/shard_map/tokens_back/pallas_call | solution.py:358
  212.5 8.6 %joint_weight.1 = (bf16[3,768,768]{2,1,0:T(8,128)(2,1)}, f32[8,768]{1,0:T(8,128)}) custom-call(bf16[1024,768]{1,0:T(8,128)(2,1)} %get-tuple-element.58.a_ref, bf16[1024,768]{1,0:T(8,128)(2,1)} %get-tuple-element.52.q_ref, bf16[1024,768]{1,0:T(8,128)(2,1)} %get-tuple-element.53.k_ref, bf16[1024,768]{1,0:T(8,128)(2,1)} %get-tuple-element.54.v_ref), custom_call_target="tpu_custom_call" | custom-call | tf_op jit(solution)/shard_map/joint_weight/pallas_call | solution.py:332
  264.3 11.1 %collective-permute-done.10 = bf16[256,768]{1,0:T(8,128)(2,1)S(1)} collective-permute-done((bf16[256,768]{1,0:T(8,128)(2,1)}, bf16[256,768]{1,0:T(8,128)(2,1)S(1)}, u32[]{:S(2)}, u32[]{:S(2)}) %collective-permute-start.10) | collective-permute-done | bytes 393248 | tf_op jit(solution)/shard_map/ppermute | solution.py:420
  292.1 7.1 %collective-permute-done.28 = bf16[384,768]{1,0:T(8,128)(2,1)S(1)} collective-permute-done((bf16[384,768]{1,0:T(8,128)(2,1)S(1)}, bf16[384,768]{1,0:T(8,128)(2,1)S(1)}, u32[]{:S(2)}, u32[]{:S(2)}) %collective-permute-start.28) | collective-permute-done | bytes 589856 | tf_op jit(solution)/shard_map/ppermute | solution.py:431
  304.1 7.6 %collective-permute-done.68 = bf16[384,768]{1,0:T(8,128)(2,1)S(1)} collective-permute-done((bf16[384,768]{1,0:T(8,128)(2,1)S(1)}, bf16[384,768]{1,0:T(8,128)(2,1)S(1)}, u32[]{:S(2)}, u32[]{:S(2)}) %collective-permute-start.68) | collective-permute-done | bytes 589856 | tf_op jit(solution)/shard_map/ppermute | solution.py:431
  316.8 7.6 %collective-permute-done.48 = bf16[384,768]{1,0:T(8,128)(2,1)S(1)} collective-permute-done((bf16[384,768]{1,0:T(8,128)(2,1)S(1)}, bf16[384,768]{1,0:T(8,128)(2,1)S(1)}, u32[]{:S(2)}, u32[]{:S(2)}) %collective-permute-start.48) | collective-permute-done | bytes 589856 | tf_op jit(solution)/shard_map/ppermute | solution.py:431
  334.8 4.9 %collective-permute-start.30 = (bf16[96,768]{1,0:T(8,128)(2,1)S(1)}, bf16[96,768]{1,0:T(8,128)(2,1)S(1)}, u32[]{:S(2)}, u32[]{:S(2)}) collective-permute-start(bf16[96,768]{1,0:T(8,128)(2,1)S(1)} %constant_dynamic-slice_fusion.20), channel_id=1, source_target_pairs={{0,1},{1,0},{2,3},{3,2},{4,5},{5,4},{6,7},{7,6},{8,9},{9,8},{10,11... | collective-permute-start | bytes 442376 | tf_op jit(solution)/shard_map/ppermute | solution.py:431
  357.1 6.1 %collective-permute-done.50 = bf16[96,768]{1,0:T(8,128)(2,1)S(1)} collective-permute-done((bf16[96,768]{1,0:T(8,128)(2,1)S(1)}, bf16[96,768]{1,0:T(8,128)(2,1)S(1)}, u32[]{:S(2)}, u32[]{:S(2)}) %collective-permute-start.50) | collective-permute-done | bytes 147488 | tf_op jit(solution)/shard_map/ppermute | solution.py:431
  369.5 5.8 %collective-permute-done.71 = bf16[48,768]{1,0:T(8,128)(2,1)S(1)} collective-permute-done((bf16[48,768]{1,0:T(8,128)(2,1)S(1)}, bf16[48,768]{1,0:T(8,128)(2,1)S(1)}, u32[]{:S(2)}, u32[]{:S(2)}) %collective-permute-start.71) | collective-permute-done | bytes 73760 | tf_op jit(solution)/shard_map/ppermute | solution.py:431
  424.7 7.9 %collective-permute-done.35 = bf16[384,768]{1,0:T(8,128)(2,1)S(1)} collective-permute-done((bf16[384,768]{1,0:T(8,128)(2,1)S(1)}, bf16[384,768]{1,0:T(8,128)(2,1)S(1)}, u32[]{:S(2)}, u32[]{:S(2)}) %collective-permute-start.35) | collective-permute-done | bytes 589856 | tf_op jit(solution)/shard_map/ppermute | solution.py:431
  439.0 12.5 %collective-permute-done.75 = bf16[384,768]{1,0:T(8,128)(2,1)S(1)} collective-permute-done((bf16[384,768]{1,0:T(8,128)(2,1)S(1)}, bf16[384,768]{1,0:T(8,128)(2,1)S(1)}, u32[]{:S(2)}, u32[]{:S(2)}) %collective-permute-start.75) | collective-permute-done | bytes 589856 | tf_op jit(solution)/shard_map/ppermute | solution.py:431
  453.5 8.1 %collective-permute-done.55 = bf16[384,768]{1,0:T(8,128)(2,1)S(1)} collective-permute-done((bf16[384,768]{1,0:T(8,128)(2,1)S(1)}, bf16[384,768]{1,0:T(8,128)(2,1)S(1)}, u32[]{:S(2)}, u32[]{:S(2)}) %collective-permute-start.55) | collective-permute-done | bytes 589856 | tf_op jit(solution)/shard_map/ppermute | solution.py:431
  (348 shorter events, 212.6 us)
Async XLA Ops:
  2.9 24.8 %collective-permute-start.3 = (bf16[256,768]{1,0:T(8,128)(2,1)}, bf16[256,768]{1,0:T(8,128)(2,1)}, u32[]{:S(2)}, u32[]{:S(2)}) collective-permute-start(bf16[256,768]{1,0:T(8,128)(2,1)} %get-tuple-element.108), channel_id=1, source_target_pairs={{0,1},{1,2},{3,0},{4,5},{5,6},{6,7},{8,9},{9,10},{11,8},{12,13},{1... | collective-permute-start | bytes 1179656 | tf_op jit(solution)/shard_map/ppermute | solution.py:401
  12.7 27.3 %collective-permute-start.4 = (bf16[256,768]{1,0:T(8,128)(2,1)}, bf16[256,768]{1,0:T(8,128)(2,1)}, u32[]{:S(2)}, u32[]{:S(2)}) collective-permute-start(bf16[256,768]{1,0:T(8,128)(2,1)} %get-tuple-element.110), channel_id=1, source_target_pairs={{0,2},{2,0},{3,1},{4,6},{5,7},{7,5},{8,10},{10,8},{11,9},{12,14},{... | collective-permute-start | bytes 1179656 | tf_op jit(solution)/shard_map/ppermute | solution.py:401
  14.6 45.3 %collective-permute-start.5 = (bf16[256,768]{1,0:T(8,128)(2,1)S(1)}, bf16[256,768]{1,0:T(8,128)(2,1)}, u32[]{:S(2)}, u32[]{:S(2)}) collective-permute-start(bf16[256,768]{1,0:T(8,128)(2,1)S(1)} %get-tuple-element.107), channel_id=1, source_target_pairs={{1,0},{2,1},{3,2},{4,7},{6,5},{7,6},{9,8},{10,9},{11,10},{12,15},{... | collective-permute-start | bytes 1179656 | tf_op jit(solution)/shard_map/ppermute | solution.py:401
  15.9 43.0 %collective-permute-start.1 = (bf16[256,768]{1,0:T(8,128)(2,1)}, bf16[256,768]{1,0:T(8,128)(2,1)}, u32[]{:S(2)}, u32[]{:S(2)}) collective-permute-start(bf16[256,768]{1,0:T(8,128)(2,1)} %get-tuple-element.114), channel_id=1, source_target_pairs={{0,2},{2,0},{3,1},{4,6},{5,7},{7,5},{8,10},{10,8},{11,9},{12,14},{... | collective-permute-start | bytes 1179656 | tf_op jit(solution)/shard_map/ppermute | solution.py:401
  27.8 32.2 %collective-permute-start.2 = (bf16[256,768]{1,0:T(8,128)(2,1)}, bf16[256,768]{1,0:T(8,128)(2,1)S(1)}, u32[]{:S(2)}, u32[]{:S(2)}) collective-permute-start(bf16[256,768]{1,0:T(8,128)(2,1)} %get-tuple-element.111), channel_id=1, source_target_pairs={{1,0},{2,1},{3,2},{4,7},{6,5},{7,6},{9,8},{10,9},{11,10},{12,15},{... | collective-permute-start | bytes 1179656 | tf_op jit(solution)/shard_map/ppermute | solution.py:401
  167.8 84.9 %collective-permute-start.8 = (bf16[256,768]{1,0:T(8,128)(2,1)}, bf16[256,768]{1,0:T(8,128)(2,1)S(1)}, u32[]{:S(2)}, u32[]{:S(2)}) collective-permute-start(bf16[256,768]{1,0:T(8,128)(2,1)} %get-tuple-element.104), channel_id=1, source_target_pairs={{0,1},{1,2},{2,3},{7,4},{5,6},{6,7},{8,9},{9,10},{10,11},{15,12},{... | collective-permute-start | bytes 1179656 | tf_op jit(solution)/shard_map/ppermute | solution.py:420
  173.3 82.9 %collective-permute-start.7 = (bf16[256,768]{1,0:T(8,128)(2,1)}, bf16[256,768]{1,0:T(8,128)(2,1)}, u32[]{:S(2)}, u32[]{:S(2)}) collective-permute-start(bf16[256,768]{1,0:T(8,128)(2,1)} %get-tuple-element.105), channel_id=1, source_target_pairs={{2,0},{0,2},{1,3},{6,4},{7,5},{5,7},{10,8},{8,10},{9,11},{14,12},{... | collective-permute-start | bytes 1179656 | tf_op jit(solution)/shard_map/ppermute | solution.py:420
  175.3 83.5 %collective-permute-start.6 = (bf16[256,768]{1,0:T(8,128)(2,1)}, bf16[256,768]{1,0:T(8,128)(2,1)}, u32[]{:S(2)}, u32[]{:S(2)}) collective-permute-start(bf16[256,768]{1,0:T(8,128)(2,1)} %get-tuple-element.106), channel_id=1, source_target_pairs={{1,0},{2,1},{0,3},{5,4},{6,5},{7,6},{9,8},{10,9},{8,11},{13,12},{1... | collective-permute-start | bytes 1179656 | tf_op jit(solution)/shard_map/ppermute | solution.py:420
  225.7 54.8 %collective-permute-start.27 = (bf16[768,768]{1,0:T(8,128)(2,1)}, bf16[768,768]{1,0:T(8,128)(2,1)}, u32[]{:S(2)}, u32[]{:S(2)}) collective-permute-start(bf16[768,768]{1,0:T(8,128)(2,1)} %constant_dynamic-slice_fusion.23), channel_id=1, source_target_pairs={{0,4},{1,5},{2,6},{3,7},{4,0},{5,1},{6,2},{7,3},{8,12},{9,13},{10,... | collective-permute-start | bytes 3538952 | tf_op jit(solution)/shard_map/ppermute | solution.py:431
  252.7 30.2 %collective-permute-start.17 = (bf16[768,768]{1,0:T(8,128)(2,1)}, bf16[768,768]{1,0:T(8,128)(2,1)}, u32[]{:S(2)}, u32[]{:S(2)}) collective-permute-start(bf16[768,768]{1,0:T(8,128)(2,1)} %constant_dynamic-slice_fusion.28), channel_id=1, source_target_pairs={{0,4},{1,5},{2,6},{3,7},{4,0},{5,1},{6,2},{7,3},{8,12},{9,13},{10,... | collective-permute-start | bytes 3538952 | tf_op jit(solution)/shard_map/ppermute | solution.py:431
  262.8 23.4 %collective-permute-start.67 = (bf16[768,768]{1,0:T(8,128)(2,1)}, bf16[768,768]{1,0:T(8,128)(2,1)S(1)}, u32[]{:S(2)}, u32[]{:S(2)}) collective-permute-start(bf16[768,768]{1,0:T(8,128)(2,1)} %constant_dynamic-slice_fusion.3), channel_id=1, source_target_pairs={{0,4},{1,5},{2,6},{3,7},{4,0},{5,1},{6,2},{7,3},{8,12},{9,13},{10,... | collective-permute-start | bytes 3538952 | tf_op jit(solution)/shard_map/ppermute | solution.py:431
  288.2 23.6 %collective-permute-start.68 = (bf16[384,768]{1,0:T(8,128)(2,1)S(1)}, bf16[384,768]{1,0:T(8,128)(2,1)S(1)}, u32[]{:S(2)}, u32[]{:S(2)}) collective-permute-start(bf16[384,768]{1,0:T(8,128)(2,1)S(1)} %constant_dynamic-slice_fusion.2), channel_id=1, source_target_pairs={{0,16},{1,17},{2,18},{3,19},{4,20},{5,21},{6,22},{7,23},{8,24},{9,... | collective-permute-start | bytes 1769480 | tf_op jit(solution)/shard_map/ppermute | solution.py:431
  289.2 25.9 %collective-permute-start.58 = (bf16[384,768]{1,0:T(8,128)(2,1)S(1)}, bf16[384,768]{1,0:T(8,128)(2,1)S(1)}, u32[]{:S(2)}, u32[]{:S(2)}) collective-permute-start(bf16[384,768]{1,0:T(8,128)(2,1)S(1)} %constant_dynamic-slice_fusion.7), channel_id=1, source_target_pairs={{0,8},{1,9},{2,10},{3,11},{4,12},{5,13},{6,14},{7,15},{8,0},{9,1},... | collective-permute-start | bytes 1769480 | tf_op jit(solution)/shard_map/ppermute | solution.py:431
  290.2 34.2 %collective-permute-start.48 = (bf16[384,768]{1,0:T(8,128)(2,1)S(1)}, bf16[384,768]{1,0:T(8,128)(2,1)S(1)}, u32[]{:S(2)}, u32[]{:S(2)}) collective-permute-start(bf16[384,768]{1,0:T(8,128)(2,1)S(1)} %constant_dynamic-slice_fusion.12), channel_id=1, source_target_pairs={{0,16},{1,17},{2,18},{3,19},{4,20},{5,21},{6,22},{7,23},{8,24},{9,... | collective-permute-start | bytes 1769480 | tf_op jit(solution)/shard_map/ppermute | solution.py:431
  299.1 28.6 %collective-permute-start.38 = (bf16[384,768]{1,0:T(8,128)(2,1)S(1)}, bf16[384,768]{1,0:T(8,128)(2,1)S(1)}, u32[]{:S(2)}, u32[]{:S(2)}) collective-permute-start(bf16[384,768]{1,0:T(8,128)(2,1)S(1)} %constant_dynamic-slice_fusion.17), channel_id=1, source_target_pairs={{0,8},{1,9},{2,10},{3,11},{4,12},{5,13},{6,14},{7,15},{8,0},{9,1},... | collective-permute-start | bytes 1769480 | tf_op jit(solution)/shard_map/ppermute | solution.py:431
  302.5 31.6 %collective-permute-start.29 = (bf16[192,768]{1,0:T(8,128)(2,1)S(1)}, bf16[192,768]{1,0:T(8,128)(2,1)S(1)}, u32[]{:S(2)}, u32[]{:S(2)}) collective-permute-start(bf16[192,768]{1,0:T(8,128)(2,1)S(1)} %constant_dynamic-slice_fusion.21), channel_id=1, source_target_pairs={{0,8},{1,9},{2,10},{3,11},{4,12},{5,13},{6,14},{7,15},{8,0},{9,1},... | collective-permute-start | bytes 884744 | tf_op jit(solution)/shard_map/ppermute | solution.py:431
  311.8 23.0 %collective-permute-start.19 = (bf16[192,768]{1,0:T(8,128)(2,1)S(1)}, bf16[192,768]{1,0:T(8,128)(2,1)S(1)}, u32[]{:S(2)}, u32[]{:S(2)}) collective-permute-start(bf16[192,768]{1,0:T(8,128)(2,1)S(1)} %constant_dynamic-slice_fusion.26), channel_id=1, source_target_pairs={{0,16},{1,17},{2,18},{3,19},{4,20},{5,21},{6,22},{7,23},{8,24},{9,... | collective-permute-start | bytes 884744 | tf_op jit(solution)/shard_map/ppermute | solution.py:431
  315.1 25.3 %collective-permute-start.69 = (bf16[192,768]{1,0:T(8,128)(2,1)S(1)}, bf16[192,768]{1,0:T(8,128)(2,1)S(1)}, u32[]{:S(2)}, u32[]{:S(2)}) collective-permute-start(bf16[192,768]{1,0:T(8,128)(2,1)S(1)} %constant_dynamic-slice_fusion.1), channel_id=1, source_target_pairs={{0,8},{1,9},{2,10},{3,11},{4,12},{5,13},{6,14},{7,15},{8,0},{9,1},... | collective-permute-start | bytes 884744 | tf_op jit(solution)/shard_map/ppermute | solution.py:431
  416.8 22.1 %collective-permute-start.44 = (bf16[192,768]{1,0:T(8,128)(2,1)S(1)}, bf16[192,768]{1,0:T(8,128)(2,1)S(1)}, u32[]{:S(2)}, u32[]{:S(2)}) collective-permute-start(bf16[192,768]{1,0:T(8,128)(2,1)S(1)} %bitcast.234), channel_id=1, source_target_pairs={{0,16},{1,17},{2,18},{3,19},{4,20},{5,21},{6,22},{7,23},{8,24},{9,... | collective-permute-start | bytes 884744 | tf_op jit(solution)/shard_map/ppermute | solution.py:431
  419.9 31.6 %collective-permute-start.75 = (bf16[384,768]{1,0:T(8,128)(2,1)S(1)}, bf16[384,768]{1,0:T(8,128)(2,1)S(1)}, u32[]{:S(2)}, u32[]{:S(2)}) collective-permute-start(bf16[384,768]{1,0:T(8,128)(2,1)S(1)} %bitcast.217), channel_id=1, source_target_pairs={{0,16},{1,17},{2,18},{3,19},{4,20},{5,21},{6,22},{7,23},{8,24},{9,... | collective-permute-start | bytes 1769480 | tf_op jit(solution)/shard_map/ppermute | solution.py:431
  423.1 30.1 %collective-permute-start.65 = (bf16[384,768]{1,0:T(8,128)(2,1)S(1)}, bf16[384,768]{1,0:T(8,128)(2,1)S(1)}, u32[]{:S(2)}, u32[]{:S(2)}) collective-permute-start(bf16[384,768]{1,0:T(8,128)(2,1)S(1)} %bitcast.219), channel_id=1, source_target_pairs={{0,8},{1,9},{2,10},{3,11},{4,12},{5,13},{6,14},{7,15},{8,0},{9,1},... | collective-permute-start | bytes 1769480 | tf_op jit(solution)/shard_map/ppermute | solution.py:431
  432.6 29.0 %collective-permute-start.55 = (bf16[384,768]{1,0:T(8,128)(2,1)S(1)}, bf16[384,768]{1,0:T(8,128)(2,1)S(1)}, u32[]{:S(2)}, u32[]{:S(2)}) collective-permute-start(bf16[384,768]{1,0:T(8,128)(2,1)S(1)} %bitcast.213), channel_id=1, source_target_pairs={{0,16},{1,17},{2,18},{3,19},{4,20},{5,21},{6,22},{7,23},{8,24},{9,... | collective-permute-start | bytes 1769480 | tf_op jit(solution)/shard_map/ppermute | solution.py:431
  435.7 29.4 %collective-permute-start.36 = (bf16[768,768]{1,0:T(8,128)(2,1)S(1)}, bf16[768,768]{1,0:T(8,128)(2,1)S(1)}, u32[]{:S(2)}, u32[]{:S(2)}) collective-permute-start(bf16[768,768]{1,0:T(8,128)(2,1)S(1)} %bitcast.197), channel_id=1, source_target_pairs={{0,4},{1,5},{2,6},{3,7},{4,0},{5,1},{6,2},{7,3},{8,12},{9,13},{10,... | collective-permute-start | bytes 3538952 | tf_op jit(solution)/shard_map/ppermute | solution.py:431
  438.9 26.7 %collective-permute-start.26 = (bf16[768,768]{1,0:T(8,128)(2,1)S(1)}, bf16[768,768]{1,0:T(8,128)(2,1)S(1)}, u32[]{:S(2)}, u32[]{:S(2)}) collective-permute-start(bf16[768,768]{1,0:T(8,128)(2,1)S(1)} %bitcast.199), channel_id=1, source_target_pairs={{0,4},{1,5},{2,6},{3,7},{4,0},{5,1},{6,2},{7,3},{8,12},{9,13},{10,... | collective-permute-start | bytes 3538952 | tf_op jit(solution)/shard_map/ppermute | solution.py:431
  (84 other events, 927.4 us)
